TPU v7x, 32 devices: a whole 2x2x4 slice. The times are simulated.
32 devices in a mesh: stn: 16 (over z, y, x), chan: 2 (over core).
Axes of the slice: x: 2, y: 2, z: 4, core: 2. Of those that a mesh axis runs over, the one named last changes fastest.
Arguments:
- voltages: bfloat16 [128, 4, 64, 128], P('stn', 'chan'), may hold values from -12 to 12
- response: bfloat16 [128, 4, 64, 128], P('stn', 'chan'), may hold values from -48 to 48
- start_gains: float32 [128, 128], replicated, may hold values from 0.5 to 1.5
- step_sizes: float32 [64], replicated, may hold values from 0.2 to 0.8
- station_ids: int32 [128], P('stn'), may hold values from 0 to 127, each once
- baseline_flags: int32 [128, 128], replicated, may hold values 0 or 1
Outputs:
- calibrated: float32 [128, 128], P('stn')
- descent: float32 [128, 128], P('stn')
Inputs may be any that keep to these rules, and one draw needn't show every extreme that they name: `station_ids`: each station number appears once. `baseline_flags`: 1 keeps a baseline, 0 flags it.
All inputs are finite; a program needn't handle non-finite values.
Results may differ from a plain program's by a relative error of at most 0.0003.
Values may be sent and summed in bfloat16 or wider, within the bound.
A program may use at most 64 MiB of HBM per device.

v0:
```python
import functools

import jax
import jax.numpy as jnp
from jax import lax
from jax.experimental import pallas as pl
from jax.experimental.pallas import tpu as pltpu
from jax.sharding import PartitionSpec as P

ITERS = 2
MESH = pl.DeviceIdType.MESH
IDS, RESP, VOLT, PAIR = 0, 1, 2, 4
SUMS = PAIR + ITERS
GATHER = SUMS + ITERS
GROUPS = GATHER + ITERS


def dot_last(left, right):
    return lax.dot_general(left, right, (((1,), (1,)), ((), ())), preferred_element_type=jnp.float32)


def dot(left, right):
    return lax.dot_general(left, right, (((1,), (0,)), ((), ())), preferred_element_type=jnp.float32)


def kernel(
    n, nchan, stations, samples,
    volt_any, resp_any, gains_any, steps_any, ids_any, flags_any,
    result_ref,
    volt_in, resp_in, gains, flags, wide_volt, wide_resp,
    volt_send, resp_send, volt_recv, resp_recv, id_rows,
    weight, a_float, a_swap, applied, observed, predicted,
    energies, chip_sum, sums, gathered, norms, current, steps_ref, ids_ref,
    in_sem, send_sem, recv_sem,
):
    everyone = n * stations
    spd = samples // n
    width = volt_in.shape[2]
    half = width // 2
    stn = lax.axis_index("stn")
    chan = lax.axis_index("chan")

    def each(first, stop, body):
        if stop - first <= 16:
            quarter = max(stop // 4, 1)
            for k in sorted(range(first, stop), key=lambda k: (k % quarter, (2, 1, 3, 0).index(k // quarter % 4))):
                body(k)
        else:
            lax.fori_loop(first, stop, lambda k, carry: (body(k), carry)[1], 0)

    def other_stations(body):
        each(1, n, lambda k: body(lax.rem(stn + k, n)))

    def other_chans(body):
        for c in range(1, nchan):
            body(lax.rem(chan + c, nchan))

    loads = [
        pltpu.make_async_copy(src, dst, in_sem.at[i])
        for i, (src, dst) in enumerate(
            (
                (ids_any, ids_ref), (resp_any, resp_in), (volt_any, volt_in),
                (flags_any, flags), (gains_any, gains), (steps_any, steps_ref),
            )
        )
    ]
    for load in loads:
        load.start()

    barrier = pltpu.get_barrier_semaphore()

    def greet(device):
        pl.semaphore_signal(barrier, inc=1, device_id=device, device_id_type=MESH)

    other_stations(lambda s: greet({"stn": s}))
    other_chans(lambda c: greet({"chan": c}))

    def wait_all(buffer, count, sem):
        part = buffer.at[pl.ds(0, count)]
        pltpu.make_async_copy(part, part, sem).wait()

    loads[0].wait()
    lane = lax.broadcasted_iota(jnp.int32, (1, everyone), 1)
    own_row = jnp.zeros((1, everyone), jnp.int32)
    for j in range(stations):
        own_row = jnp.where(lane == stn * stations + j, ids_ref[j], own_row)
    id_rows[stn] = own_row

    loads[1].wait()
    wide_resp[...] = resp_in[...].astype(jnp.float32).reshape(stations * samples, width)

    def pack(wide, send, dst, pairs):
        for pair in pairs:
            first = dst * spd + 2 * pair
            both = jnp.concatenate(
                [wide[pl.ds(first + j, stations, stride=samples), :] for j in range(2)], axis=0
            )
            send[dst, pl.ds(2 * pair * stations, 2 * stations), :] = both.astype(jnp.bfloat16)

    def remote(src, dst_ref, group, device):
        pltpu.make_async_remote_copy(
            src_ref=src, dst_ref=dst_ref, send_sem=send_sem.at[group],
            recv_sem=recv_sem.at[group], device_id=device, device_id_type=MESH,
        ).start()

    pairs = spd // 2
    chunks = 2 if pairs > 1 else 1
    chunk_pairs = [range(pairs - 1), range(pairs - 1, pairs)][2 - chunks:]
    chunk_rows = [
        pl.ds(2 * part.start * stations, 2 * len(part) * stations) for part in chunk_pairs
    ]

    pl.semaphore_wait(barrier, n + nchan - 2)

    def send_resp(dst):
        remote(id_rows.at[stn], id_rows.at[stn], IDS, {"stn": dst})
        pack(wide_resp, resp_send, dst, range(pairs))
        remote(resp_send.at[dst], resp_recv.at[stn], RESP, {"stn": dst})

    other_stations(send_resp)
    loads[2].wait()
    wide_volt[...] = volt_in[...].astype(jnp.float32).reshape(stations * samples, width)
    for chunk in range(chunks):

        def send_volt(dst, chunk=chunk):
            pack(wide_volt, volt_send, dst, chunk_pairs[chunk])
            part = chunk_rows[chunk]
            remote(volt_send.at[dst, part], volt_recv.at[stn, part], VOLT + chunk, {"stn": dst})

        other_stations(send_volt)
    pack(wide_resp, resp_send, stn, range(pairs))
    resp_recv[stn] = resp_send[stn]
    pack(wide_volt, volt_send, stn, range(pairs))
    volt_recv[stn] = volt_send[stn]

    loads[3].wait()
    flag = flags[...].astype(jnp.float32)
    mutual = (flag * flag.T).astype(jnp.bfloat16)
    wait_all(id_rows, n - 1, recv_sem.at[IDS])
    all_ids = jnp.sum(id_rows[...], axis=0)
    row = lax.broadcasted_iota(jnp.int32, (everyone, everyone), 0)
    column = lax.broadcasted_iota(jnp.int32, (everyone, everyone), 1)
    one_hot = (row == all_ids).astype(jnp.float32).astype(jnp.bfloat16)
    picked = dot(mutual, one_hot).T.astype(jnp.bfloat16)
    weight[...] = jnp.where(row == column, 0.0, dot(picked, one_hot))

    def unpack(recv, pair):
        block = recv[:, pl.ds(2 * pair * stations, 2 * stations), :].astype(jnp.float32)
        block = block.reshape(n, 2, stations, width)
        return [block[:, j].reshape(everyone, width) for j in range(2)]

    sign = jnp.where(lax.broadcasted_iota(jnp.int32, (1, width), 1) < half, -1.0, 1.0)
    loads[4].wait()
    loads[5].wait()
    steps = steps_ref[...].reshape(1, half)
    steps = jnp.concatenate([steps, steps], axis=1)

    def predict(t, gain_both, gain_turn):
        a = a_float[t]
        turned = gain_both * a + gain_turn * a_swap[t]
        applied[t, pl.ds(0, everyone), :] = turned.astype(jnp.bfloat16)
        applied[t, pl.ds(everyone, everyone), :] = (sign * pltpu.roll(turned, half, 1)).astype(jnp.bfloat16)
        return dot_last(applied[t, pl.ds(0, everyone), :], applied[t])

    def gain_parts(gain):
        swapped = pltpu.roll(gain, half, 1)
        left = sign < 0.0
        return jnp.where(left, gain, swapped), jnp.where(left, -swapped, gain)

    wait_all(resp_recv, n - 1, recv_sem.at[RESP])
    gain_both, gain_turn = gain_parts(gains[...])
    for pair in range(spd // 2):
        for j, a in enumerate(unpack(resp_recv, pair)):
            t = 2 * pair + j
            a_float[t] = a
            a_swap[t] = pltpu.roll(a, half, 1)
            predicted[t] = predict(t, gain_both, gain_turn)

    def accumulate(t, left_over, totals):
        residual = jnp.concatenate(
            [
                (weight[...] * left_over[:, :everyone]).astype(jnp.bfloat16),
                (weight[...] * left_over[:, everyone:]).astype(jnp.bfloat16),
            ],
            axis=1,
        )
        hidden = dot(residual, applied[t])
        return totals[0] + a_float[t] * hidden, totals[1] + a_swap[t] * hidden

    def volt_chunk(chunk):
        part = volt_recv.at[pl.ds(0, n - 1), chunk_rows[chunk]]
        return pltpu.make_async_copy(part, part, recv_sem.at[VOLT + chunk])

    for iteration in range(ITERS):
        totals = (jnp.zeros((everyone, width), jnp.float32), jnp.zeros((everyone, width), jnp.float32))
        if iteration == 0:
            for chunk in range(chunks):
                volt_chunk(chunk).wait()
                for pair in chunk_pairs[chunk]:
                    for j, x in enumerate(unpack(volt_recv, pair)):
                        t = 2 * pair + j
                        mine = x.astype(jnp.bfloat16)
                        turned = (sign * pltpu.roll(x, half, 1)).astype(jnp.bfloat16)
                        seen = dot_last(mine, jnp.concatenate([mine, turned], axis=0))
                        observed[t] = seen
                        totals = accumulate(t, seen - predicted[t], totals)
        else:
            gain_both, gain_turn = gain_parts(current[...])
            left_over = observed[0] - predict(0, gain_both, gain_turn)
            for t in range(spd):
                held_over = left_over
                if t + 1 < spd:
                    left_over = observed[t + 1] - predict(t + 1, gain_both, gain_turn)
                totals = accumulate(t, held_over, totals)
        direct, crossed = totals
        energy = jnp.where(
            sign < 0.0,
            direct + pltpu.roll(direct, half, 1),
            crossed - pltpu.roll(crossed, half, 1),
        )
        energies[iteration, chan] = energy.reshape(n, stations, width)
        mine = energies.at[iteration, chan]
        other_chans(lambda c: remote(mine, mine, PAIR + iteration, {"chan": c}))
        wait_all(energies.at[iteration], nchan - 1, recv_sem.at[PAIR + iteration])
        chip_sum[iteration] = jnp.sum(energies[iteration], axis=0)
        other_stations(
            lambda s: remote(
                chip_sum.at[iteration, s], sums.at[iteration, stn], SUMS + iteration, {"stn": s}
            )
        )
        sums[iteration, stn] = chip_sum[iteration, stn]
        wait_all(sums.at[iteration], n - 1, recv_sem.at[SUMS + iteration])
        scale = -(2.0 / half) / half
        block = scale * jnp.sum(sums[iteration], axis=0)
        if iteration < ITERS - 1:
            gathered[iteration, stn] = block
            part = gathered.at[iteration, stn]
            other_stations(lambda s: remote(part, part, GATHER + iteration, {"stn": s}))
            wait_all(gathered.at[iteration], n - 1, recv_sem.at[GATHER + iteration])
            gradient = gathered[iteration].reshape(everyone, width)
            spread = jnp.sqrt(jnp.sum(gradient * gradient, keepdims=True) / (everyone * half) + 1e-06)
            held = gains if iteration == 0 else current
            current[...] = held[...] - steps * (gradient / spread)
        else:
            norms[stn] = jnp.sum(block * block, axis=0, keepdims=True)
            part = norms.at[stn]
            other_stations(lambda s: remote(part, part, GATHER + iteration, {"stn": s}))
            own = current[pl.ds(pl.multiple_of(stn * stations, stations), stations), :]
            wait_all(norms, n - 1, recv_sem.at[GATHER + iteration])
            total = jnp.sum(jnp.sum(norms[...], axis=0), keepdims=True)
            spread = jnp.sqrt(total / (everyone * half) + 1e-06)
            descent = block / spread
            result_ref[0] = own - steps * descent
            result_ref[1] = descent

    wait_all(id_rows, n - 1, send_sem.at[IDS])
    wait_all(resp_send, n - 1, send_sem.at[RESP])
    for chunk in range(chunks):
        part = volt_send.at[pl.ds(0, n - 1), chunk_rows[chunk]]
        pltpu.make_async_copy(part, part, send_sem.at[VOLT + chunk]).wait()
    for iteration in range(ITERS):
        wait_all(energies.at[iteration], nchan - 1, send_sem.at[PAIR + iteration])
        wait_all(sums.at[iteration], n - 1, send_sem.at[SUMS + iteration])
        last = gathered.at[iteration] if iteration < ITERS - 1 else norms
        wait_all(last, n - 1, send_sem.at[GATHER + iteration])


def shards(n, nchan, voltages, response, start_gains, step_sizes, station_ids, baseline_flags):
    stations, width = voltages.shape[0], voltages.shape[3]
    samples = voltages.shape[1] * voltages.shape[2]
    everyone = stations * n
    spd = samples // n
    half = width // 2
    f32, bf16 = jnp.float32, jnp.bfloat16
    hbm = pl.BlockSpec(memory_space=pltpu.HBM)
    vmem = pl.BlockSpec(memory_space=pltpu.VMEM)
    block = (n, spd * stations, width)
    scratch = [
        ((stations, samples, width), bf16),
        ((stations, samples, width), bf16),
        ((everyone, width), f32),
        ((everyone, everyone), jnp.int32),
        ((stations * samples, width), f32),
        ((stations * samples, width), f32),
        (block, bf16),
        (block, bf16),
        (block, bf16),
        (block, bf16),
        ((n, 1, everyone), jnp.int32),
        ((everyone, everyone), f32),
        ((spd, everyone, width), f32),
        ((spd, everyone, width), f32),
        ((spd, 2 * everyone, width), bf16),
        ((spd, everyone, 2 * everyone), f32),
        ((spd, everyone, 2 * everyone), f32),
        ((ITERS, nchan, n, stations, width), f32),
        ((ITERS, n, stations, width), f32),
        ((ITERS, n, stations, width), f32),
        ((ITERS - 1, n, stations, width), f32),
        ((n, 1, width), f32),
        ((everyone, width), f32),
        ((half,), f32),
    ]
    result = pl.pallas_call(
        functools.partial(kernel, n, nchan, stations, samples),
        out_shape=jax.ShapeDtypeStruct((2, stations, width), f32),
        in_specs=[hbm] * 6,
        out_specs=vmem,
        scratch_shapes=[pltpu.VMEM(shape, dtype) for shape, dtype in scratch]
        + [pltpu.SMEM((stations,), jnp.int32), pltpu.SemaphoreType.DMA((6,)), pltpu.SemaphoreType.DMA((GROUPS,)), pltpu.SemaphoreType.DMA((GROUPS,))],
        compiler_params=pltpu.CompilerParams(
            collective_id=0, has_side_effects=True, vmem_limit_bytes=64 * 1024 * 1024
        ),
    )(
        voltages.reshape(stations, samples, width),
        response.reshape(stations, samples, width),
        start_gains, step_sizes, station_ids, baseline_flags,
    )
    return result[0], result[1]


def solution(mesh):
    placed = (P("stn", "chan", None, None), P("stn", "chan", None, None), P(), P(), P("stn"), P())
    return jax.shard_map(
        functools.partial(shards, mesh.shape["stn"], mesh.shape["chan"]),
        mesh=mesh,
        in_specs=placed,
        out_specs=(P("stn", None), P("stn", None)),
        check_vma=False,
    )
```

profile of v0, /device:TPU:0, one launch (start us, length us, event | category | flops | bytes accessed | tf_op | source)
XLA Modules:
  0.0 43.3 jit_solution(10526926147278075538)
XLA Ops:
  0.6 41.4 %shard_map.77 = f32[2,8,128]{2,1,0:T(8,128)} custom-call(bf16[8,128,128]{2,1,0:T(8,128)(2,1)} %bitcast.6, bf16[8,128,128]{2,1,0:T(8,128)(2,1)} %bitcast.7, f32[128,128]{1,0:T(8,128)} %gains_any.1, f32[64]{0:T(128)} %steps_any.1, s32[8]{0:T(128)} %ids_any.1, s32[128,128]{1,0:T(8,128)} %flags_any.1), custom_call_target="tpu_custom_call" | custom-call | tf_op jit(solution)/shard_map/pallas_call | solution.py:304
  42.0 1.3 %slice_bitcast_fusion = (f32[8,128]{1,0:T(8,128)}, f32[8,128]{1,0:T(8,128)}) fusion(f32[2,8,128]{2,1,0:T(8,128)} %shard_map.77), kind=kLoop, calls=%fused_computation | loop fusion | bytes 16384 | tf_op jit(solution)/shard_map/squeeze | solution.py:319
where the time goes:
time: 43.5 us; the launch traced here: 43.3 us
  Pallas kernels  41.4 us (95%)
  local copies, waits for them, and re-layouts  1.28 us (3%)
  between operations  0.64 us (1%)
    pallas_call x1, Pallas kernels, shards(): pl.pallas_call(functools.partial(kernel, n, nchan, stations, samples), ou...  41.4 us
    squeeze x1, local copies, waits for them, and re-layouts, shards(): return (result[0], result[1])  1.28 us

commit v1 on v0

--- a/solution.py
+++ b/solution.py
@@ -55,6 +55,14 @@
         for c in range(1, nchan):
             body(lax.rem(chan + c, nchan))
 
+    barrier = pltpu.get_barrier_semaphore()
+
+    def greet(device):
+        pl.semaphore_signal(barrier, inc=1, device_id=device, device_id_type=MESH)
+
+    other_stations(lambda s: greet({"stn": s}))
+    other_chans(lambda c: greet({"chan": c}))
+
     loads = [
         pltpu.make_async_copy(src, dst, in_sem.at[i])
         for i, (src, dst) in enumerate(
@@ -67,14 +75,6 @@
     for load in loads:
         load.start()
 
-    barrier = pltpu.get_barrier_semaphore()
-
-    def greet(device):
-        pl.semaphore_signal(barrier, inc=1, device_id=device, device_id_type=MESH)
-
-    other_stations(lambda s: greet({"stn": s}))
-    other_chans(lambda c: greet({"chan": c}))
-
     def wait_all(buffer, count, sem):
         part = buffer.at[pl.ds(0, count)]
         pltpu.make_async_copy(part, part, sem).wait()
@@ -113,11 +113,11 @@
     pl.semaphore_wait(barrier, n + nchan - 2)
 
     def send_resp(dst):
-        remote(id_rows.at[stn], id_rows.at[stn], IDS, {"stn": dst})
         pack(wide_resp, resp_send, dst, range(pairs))
         remote(resp_send.at[dst], resp_recv.at[stn], RESP, {"stn": dst})
 
     other_stations(send_resp)
+    other_stations(lambda s: remote(id_rows.at[stn], id_rows.at[stn], IDS, {"stn": s}))
     loads[2].wait()
     wide_volt[...] = volt_in[...].astype(jnp.float32).reshape(stations * samples, width)
     for chunk in range(chunks):

time: 43.5 us -> 43.4 us (level)
  no operation moved by 1% of the time
where the time goes in v1:
time: 43.4 us; the launch traced here: 43.2 us
  Pallas kernels  41.3 us (95%)
  local copies, waits for them, and re-layouts  1.28 us (3%)
  between operations  0.64 us (1%)
    pallas_call x1, Pallas kernels, shards(): pl.pallas_call(functools.partial(kernel, n, nchan, stations, samples), ou...  41.3 us
    squeeze x1, local copies, waits for them, and re-layouts, shards(): return (result[0], result[1])  1.28 us

profile of v1, /device:TPU:0, one launch (start us, length us, event | category | flops | bytes accessed | tf_op | source)
XLA Modules:
  0.0 43.2 jit_solution(6287329174189772118)
XLA Ops:
  0.6 41.3 %shard_map.77 = f32[2,8,128]{2,1,0:T(8,128)} custom-call(bf16[8,128,128]{2,1,0:T(8,128)(2,1)} %bitcast.6, bf16[8,128,128]{2,1,0:T(8,128)(2,1)} %bitcast.7, f32[128,128]{1,0:T(8,128)} %gains_any.1, f32[64]{0:T(128)} %steps_any.1, s32[8]{0:T(128)} %ids_any.1, s32[128,128]{1,0:T(8,128)} %flags_any.1), custom_call_target="tpu_custom_call" | custom-call | tf_op jit(solution)/shard_map/pallas_call | solution.py:304
  41.9 1.3 %slice_bitcast_fusion = (f32[8,128]{1,0:T(8,128)}, f32[8,128]{1,0:T(8,128)}) fusion(f32[2,8,128]{2,1,0:T(8,128)} %shard_map.77), kind=kLoop, calls=%fused_computation | loop fusion | bytes 16384 | tf_op jit(solution)/shard_map/squeeze | solution.py:319

commit v2 on v1

--- a/solution.py
+++ b/solution.py
@@ -37,6 +37,7 @@
     spd = samples // n
     width = volt_in.shape[2]
     half = width // 2
+    pitch = samples + 8
     stn = lax.axis_index("stn")
     chan = lax.axis_index("chan")
 
@@ -87,13 +88,14 @@
     id_rows[stn] = own_row
 
     loads[1].wait()
-    wide_resp[...] = resp_in[...].astype(jnp.float32).reshape(stations * samples, width)
+    for p in range(stations):
+        wide_resp[pl.ds(p * pitch, samples), :] = resp_in[p].astype(jnp.float32)
 
     def pack(wide, send, dst, pairs):
         for pair in pairs:
             first = dst * spd + 2 * pair
             both = jnp.concatenate(
-                [wide[pl.ds(first + j, stations, stride=samples), :] for j in range(2)], axis=0
+                [wide[pl.ds(first + j, stations, stride=pitch), :] for j in range(2)], axis=0
             )
             send[dst, pl.ds(2 * pair * stations, 2 * stations), :] = both.astype(jnp.bfloat16)
 
@@ -119,7 +121,8 @@
     other_stations(send_resp)
     other_stations(lambda s: remote(id_rows.at[stn], id_rows.at[stn], IDS, {"stn": s}))
     loads[2].wait()
-    wide_volt[...] = volt_in[...].astype(jnp.float32).reshape(stations * samples, width)
+    for p in range(stations):
+        wide_volt[pl.ds(p * pitch, samples), :] = volt_in[p].astype(jnp.float32)
     for chunk in range(chunks):
 
         def send_volt(dst, chunk=chunk):
@@ -280,8 +283,8 @@
         ((stations, samples, width), bf16),
         ((everyone, width), f32),
         ((everyone, everyone), jnp.int32),
-        ((stations * samples, width), f32),
-        ((stations * samples, width), f32),
+        ((stations * (samples + 8), width), f32),
+        ((stations * (samples + 8), width), f32),
         (block, bf16),
         (block, bf16),
         (block, bf16),

time: 43.4 us -> 43.4 us (level)
  no operation moved by 1% of the time
where the time goes in v2:
time: 43.4 us; the launch traced here: 43.2 us
  Pallas kernels  41.3 us (95%)
  local copies, waits for them, and re-layouts  1.28 us (3%)
  between operations  0.64 us (1%)
    pallas_call x1, Pallas kernels, shards(): pl.pallas_call(functools.partial(kernel, n, nchan, stations, samples), ou...  41.3 us
    squeeze x1, local copies, waits for them, and re-layouts, shards(): return (result[0], result[1])  1.28 us

profile of v2, /device:TPU:0, one launch (start us, length us, event | category | flops | bytes accessed | tf_op | source)
XLA Modules:
  0.0 43.2 jit_solution(16774525581825469023)
XLA Ops:
  0.6 41.3 %shard_map.77 = f32[2,8,128]{2,1,0:T(8,128)} custom-call(bf16[8,128,128]{2,1,0:T(8,128)(2,1)} %bitcast.6, bf16[8,128,128]{2,1,0:T(8,128)(2,1)} %bitcast.7, f32[128,128]{1,0:T(8,128)} %gains_any.1, f32[64]{0:T(128)} %steps_any.1, s32[8]{0:T(128)} %ids_any.1, s32[128,128]{1,0:T(8,128)} %flags_any.1), custom_call_target="tpu_custom_call" | custom-call | tf_op jit(solution)/shard_map/pallas_call | solution.py:307
  41.9 1.3 %slice_bitcast_fusion = (f32[8,128]{1,0:T(8,128)}, f32[8,128]{1,0:T(8,128)}) fusion(f32[2,8,128]{2,1,0:T(8,128)} %shard_map.77), kind=kLoop, calls=%fused_computation | loop fusion | bytes 16384 | tf_op jit(solution)/shard_map/squeeze | solution.py:322
